TPU v7x, 32 devices: a whole 2x2x4 slice. The times are simulated.
32 devices in a mesh: section: 4 (over z), tm: 4 (over y, x), batch: 2 (over core).
Axes of the slice: x: 2, y: 2, z: 4, core: 2. Of those that a mesh axis runs over, the one named last changes fastest.
Arguments:
- acts: bfloat16 [4, 4, 8, 6, 10240], P('section', 'batch', 'tm'), may hold values from -6 to 6
- cot: bfloat16 [4, 8, 6, 10240], P('batch', 'tm'), may hold values from -6 to 6
- spatial_weight: bfloat16 [4, 9, 64, 64], P('section'), may hold values from -0.25 to 0.25
- temporal_weight: bfloat16 [4, 3, 64, 64], P('section'), may hold values from -0.4375 to 0.4375
Outputs:
- grad_in: bfloat16 [4, 4, 8, 6, 10240], P('section', 'batch', 'tm')
- grad_spatial: float32 [4, 9, 64, 64], P('section')
- grad_temporal: float32 [4, 3, 64, 64], P('section')
All inputs are finite; a program needn't handle non-finite values.
Results may differ from a plain program's by a relative error of at most 0.012.
Values may be sent and summed in bfloat16 or wider, within the bound.
A program may use at most 128 MiB of HBM per device.

v0:
```python
import jax
import jax.numpy as jnp
from jax import lax
from jax.sharding import PartitionSpec as P

TIME_DILATION = 2


def from_behind(value, axis, steps):
    count = lax.axis_size(axis)
    first, last = (max(0, -steps), min(count, count - steps))
    return lax.ppermute(value, axis, [(source, source + steps) for source in range(first, last)])


def split_pixels(a, chans):
    return a.reshape(a.shape[:-1] + (a.shape[-1] // chans, chans))


def paired_kernel(kernel):
    return jnp.kron(jnp.eye(2, dtype=kernel.dtype), kernel)


def spatial_fwd(x, ws):
    rows, width = (x.shape[1], x.shape[2])
    chans = ws.shape[-1]
    padded = jnp.pad(x, ((0, 0), (1, 1), (chans, chans)))
    total = jnp.zeros(x.shape, jnp.float32)
    for i in range(3):
        for j in range(3):
            piece = split_pixels(padded[:, i : i + rows, j * chans : j * chans + width], 2 * chans)
            total = total + jnp.einsum(
                "nrpa,ab->nrpb",
                piece,
                paired_kernel(ws[3 * i + j]),
                preferred_element_type=jnp.float32,
            ).reshape(x.shape)
    return total


def spatial_back(gz, x, ws):
    rows, width = (x.shape[1], x.shape[2])
    chans = ws.shape[-1]
    xpad = jnp.pad(x, ((0, 0), (1, 1), (chans, chans)))
    gradient_padded = jnp.pad(gz, ((0, 0), (1, 1), (chans, chans)))
    gz_pairs = split_pixels(gz, 2 * chans)
    total = jnp.zeros(x.shape, jnp.float32)
    grads = []
    for i in range(3):
        for j in range(3):
            gpiece = split_pixels(
                gradient_padded[:, 2 - i : 2 - i + rows, (2 - j) * chans : (2 - j) * chans + width],
                2 * chans,
            )
            total = total + jnp.einsum(
                "nrpb,ab->nrpa",
                gpiece,
                paired_kernel(ws[3 * i + j]),
                preferred_element_type=jnp.float32,
            ).reshape(x.shape)
            xpiece = split_pixels(xpad[:, i : i + rows, j * chans : j * chans + width], 2 * chans)
            square = jnp.einsum(
                "nrpa,nrpb->ab", xpiece, gz_pairs, preferred_element_type=jnp.float32
            )
            grads.append(square[:chans, :chans] + square[chans:, chans:])
    return (total, jnp.stack(grads))


def temporal_back(h, gradient_piece, gradient_padded, dilation_step, wt):
    count = gradient_piece.shape[0]
    chans = wt.shape[-1]
    kernel_taps = [
        gradient_padded[2 * dilation_step : 2 * dilation_step + count],
        gradient_piece,
        gradient_padded[0:count],
    ]
    h_pix = split_pixels(h, chans)
    gh = jnp.zeros(gradient_piece.shape, jnp.float32)
    tgrads = []
    for k in range(3):
        tap = split_pixels(kernel_taps[k], chans)
        gh = gh + jnp.einsum(
            "trwd,cd->trwc", tap, wt[k], preferred_element_type=jnp.float32
        ).reshape(gradient_piece.shape)
        tgrads.append(jnp.einsum("trwc,trwd->cd", h_pix, tap, preferred_element_type=jnp.float32))
    return (gh.astype(jnp.bfloat16), jnp.stack(tgrads))


def section_backward(x, gradient_piece, ws, wt):
    dilation_step = TIME_DILATION
    z = spatial_fwd(x, ws)
    sig = jax.nn.sigmoid(z)
    h = (z * sig).astype(jnp.bfloat16)
    deriv = sig * (1.0 + z * (1.0 - sig))
    tile_gradient, h_tile = (
        lax.all_to_all(gradient_piece, "tm", split_axis=2, concat_axis=0, tiled=True),
        lax.all_to_all(h, "tm", split_axis=2, concat_axis=0, tiled=True),
    )
    gradient_padded = jnp.pad(tile_gradient, ((dilation_step, dilation_step), (0, 0), (0, 0)))
    gh_tile, tgrads = temporal_back(h_tile, tile_gradient, gradient_padded, dilation_step, wt)
    gh = lax.all_to_all(gh_tile, "tm", split_axis=0, concat_axis=2, tiled=True)
    gz = (gh.astype(jnp.float32) * deriv).astype(jnp.bfloat16)
    back, sgrads = spatial_back(gz, x, ws)
    result = (gradient_piece.astype(jnp.float32) + back).astype(jnp.bfloat16)
    return (result, sgrads, tgrads)


def body(acts, cot, spatial_weight, temporal_weight):
    section_idx = lax.axis_index("section")
    number_sections = lax.axis_size("section")
    micro = acts.shape[1]
    local_acts = acts[0]
    ws = spatial_weight[0]
    wt = temporal_weight[0]
    received = jnp.zeros(cot.shape[1:], jnp.bfloat16)
    grads_in = jnp.zeros(local_acts.shape, jnp.bfloat16)
    acc_spatial = jnp.zeros(ws.shape, jnp.float32)
    acc_temporal = jnp.zeros(wt.shape, jnp.float32)
    total_turns = micro + number_sections - 1
    for turn in range(total_turns):
        which = jnp.int32(turn) - (number_sections - 1 - section_idx)
        valid = jnp.logical_and(which >= 0, which < micro)
        clipped = jnp.clip(which, 0, micro - 1)
        x_now = lax.dynamic_index_in_dim(local_acts, clipped, 0, keepdims=False)
        top_grad = lax.dynamic_index_in_dim(cot, clipped, 0, keepdims=False)
        incoming = jnp.where(section_idx == number_sections - 1, top_grad, received)
        result, sgrads, tgrads = section_backward(x_now, incoming, ws, wt)
        weight = valid.astype(jnp.float32)
        acc_spatial = acc_spatial + weight * sgrads
        acc_temporal = acc_temporal + weight * tgrads
        select = (jnp.arange(micro, dtype=jnp.int32) == which)[:, None, None, None]
        grads_in = jnp.where(select, result[None], grads_in)
        if turn + 1 < total_turns:
            received = from_behind(result, "section", -1)
    sum_spatial, sum_temporal = lax.psum((acc_spatial, acc_temporal), ("tm", "batch"))
    return (grads_in[None], sum_spatial[None], sum_temporal[None])


def solution(mesh):
    in_specs = (
        P("section", "batch", "tm", None, None),
        P("batch", "tm", None, None),
        P("section", None, None, None),
        P("section", None, None, None),
    )
    out_specs = (
        P("section", "batch", "tm", None, None),
        P("section", None, None, None),
        P("section", None, None, None),
    )
    return jax.shard_map(body, mesh=mesh, in_specs=in_specs, out_specs=out_specs, check_vma=False)
```

profile of v0, /device:TPU:24, one launch (start us, length us, event | category | flops | bytes accessed | tf_op | source)
XLA Modules:
  0.0 929.5 jit_solution(14927379624928204376)
XLA Ops:
  8.3 8.2 copy.623
  16.6 10.0 %reshape.1685 = bf16[4,2,15360]{2,1,0:T(2,128)(2,1)} reshape(bf16[10240,2,6]{2,1,0:T(2,128)(2,1)} %bitcast.1159) | data formatting | bytes 491520
  26.5 4.2 all-to-all-start
  126.4 13.6 %reshape.1686 = bf16[10240,2,6]{2,1,0:T(2,128)(2,1)} reshape(bf16[4,2,15360]{2,1,0:T(2,128)(2,1)} %all-to-all-done) | data formatting | bytes 491520
  140.0 10.6 %copy.624 = bf16[2,6,4,2560]{3,0,2,1:T(2,128)(2,1)S(1)} copy(bf16[2,6,4,2560]{1,0,3,2:T(2,128)(2,1)} %bitcast.1160) | data formatting | bytes 491520 | tf_op jit(solution)/shard_map/all_to_all | solution.py:95
  153.7 4.3 all-to-all-start.1
  159.1 4.6 all-to-all-done.1
  205.2 10.3 %copy.809 = bf16[2,6,10240]{1,0,2:T(2,128)(2,1)} copy(bf16[2,6,10240]{2,0,1:T(2,128)(2,1)} %get-tuple-element.11) | data formatting | bytes 491520 | tf_op jit(solution)/shard_map/convert_element_type | solution.py:92
  215.5 9.9 %reshape.1695 = bf16[4,2,15360]{2,1,0:T(2,128)(2,1)} reshape(bf16[10240,2,6]{2,1,0:T(2,128)(2,1)} %bitcast.1161) | data formatting | bytes 491520
  233.9 8.2 copy.651
  242.1 9.9 %reshape.1687 = bf16[4,2,15360]{2,1,0:T(2,128)(2,1)} reshape(bf16[10240,2,6]{2,1,0:T(2,128)(2,1)} %bitcast.1175) | data formatting | bytes 491520
  257.1 12.6 %reshape.1696 = bf16[10240,2,6]{2,1,0:T(2,128)(2,1)} reshape(bf16[4,2,15360]{2,1,0:T(2,128)(2,1)S(1)} %all-to-all-done.10) | data formatting | bytes 491520
  269.7 12.2 %copy.902 = bf16[2,6,4,2560]{3,2,0,1:T(4,128)(2,1)S(1)} copy(bf16[2,6,4,2560]{1,0,3,2:T(2,128)(2,1)} %bitcast.1162) | data formatting | bytes 491520 | tf_op jit(solution)/shard_map/all_to_all | solution.py:96
  283.3 12.6 %reshape.1688 = bf16[10240,2,6]{2,1,0:T(2,128)(2,1)} reshape(bf16[4,2,15360]{2,1,0:T(2,128)(2,1)S(1)} %all-to-all-done.2) | data formatting | bytes 491520
  296.0 10.2 %copy.652 = bf16[2,6,4,2560]{3,0,2,1:T(2,128)(2,1)S(1)} copy(bf16[2,6,4,2560]{1,0,3,2:T(2,128)(2,1)} %bitcast.1163) | data formatting | bytes 491520 | tf_op jit(solution)/shard_map/all_to_all | solution.py:95
  314.8 4.4 all-to-all-start.3
  366.4 10.3 %copy.812 = bf16[2,6,10240]{1,0,2:T(2,128)(2,1)} copy(bf16[2,6,10240]{2,0,1:T(2,128)(2,1)} %get-tuple-element.9) | data formatting | bytes 491520 | tf_op jit(solution)/shard_map/convert_element_type | solution.py:92
  376.7 9.9 %reshape.1697 = bf16[4,2,15360]{2,1,0:T(2,128)(2,1)} reshape(bf16[10240,2,6]{2,1,0:T(2,128)(2,1)} %bitcast.1164) | data formatting | bytes 491520
  395.5 8.1 copy.679
  403.7 9.9 %reshape.1689 = bf16[4,2,15360]{2,1,0:T(2,128)(2,1)} reshape(bf16[10240,2,6]{2,1,0:T(2,128)(2,1)} %bitcast.1176) | data formatting | bytes 491520
  418.4 12.6 %reshape.1698 = bf16[10240,2,6]{2,1,0:T(2,128)(2,1)} reshape(bf16[4,2,15360]{2,1,0:T(2,128)(2,1)S(1)} %all-to-all-done.11) | data formatting | bytes 491520
  431.1 12.2 %copy.903 = bf16[2,6,4,2560]{3,2,0,1:T(4,128)(2,1)S(1)} copy(bf16[2,6,4,2560]{1,0,3,2:T(2,128)(2,1)} %bitcast.1165) | data formatting | bytes 491520 | tf_op jit(solution)/shard_map/all_to_all | solution.py:96
  444.7 12.6 %reshape.1690 = bf16[10240,2,6]{2,1,0:T(2,128)(2,1)} reshape(bf16[4,2,15360]{2,1,0:T(2,128)(2,1)S(1)} %all-to-all-done.4) | data formatting | bytes 491520
  457.3 10.2 %copy.680 = bf16[2,6,4,2560]{3,0,2,1:T(2,128)(2,1)S(1)} copy(bf16[2,6,4,2560]{1,0,3,2:T(2,128)(2,1)} %bitcast.1166) | data formatting | bytes 491520 | tf_op jit(solution)/shard_map/all_to_all | solution.py:95
  476.2 4.4 all-to-all-start.5
  525.7 10.2 %copy.815 = bf16[2,6,10240]{1,0,2:T(2,128)(2,1)} copy(bf16[2,6,10240]{2,0,1:T(2,128)(2,1)} %get-tuple-element.7) | data formatting | bytes 491520 | tf_op jit(solution)/shard_map/convert_element_type | solution.py:92
  536.0 9.9 %reshape.1699 = bf16[4,2,15360]{2,1,0:T(2,128)(2,1)} reshape(bf16[10240,2,6]{2,1,0:T(2,128)(2,1)} %bitcast.1167) | data formatting | bytes 491520
  554.6 8.1 copy.707
  562.8 9.9 %reshape.1691 = bf16[4,2,15360]{2,1,0:T(2,128)(2,1)} reshape(bf16[10240,2,6]{2,1,0:T(2,128)(2,1)} %bitcast.1177) | data formatting | bytes 491520
  577.8 12.6 %reshape.1700 = bf16[10240,2,6]{2,1,0:T(2,128)(2,1)} reshape(bf16[4,2,15360]{2,1,0:T(2,128)(2,1)S(1)} %all-to-all-done.12) | data formatting | bytes 491520
  590.4 12.2 %copy.904 = bf16[2,6,4,2560]{3,2,0,1:T(4,128)(2,1)S(1)} copy(bf16[2,6,4,2560]{1,0,3,2:T(2,128)(2,1)} %bitcast.1168) | data formatting | bytes 491520 | tf_op jit(solution)/shard_map/all_to_all | solution.py:96
  604.0 12.6 %reshape.1692 = bf16[10240,2,6]{2,1,0:T(2,128)(2,1)} reshape(bf16[4,2,15360]{2,1,0:T(2,128)(2,1)S(1)} %all-to-all-done.6) | data formatting | bytes 491520
  616.6 10.2 %copy.708 = bf16[2,6,4,2560]{3,0,2,1:T(2,128)(2,1)S(1)} copy(bf16[2,6,4,2560]{1,0,3,2:T(2,128)(2,1)} %bitcast.1169) | data formatting | bytes 491520 | tf_op jit(solution)/shard_map/all_to_all | solution.py:95
  635.5 4.6 all-to-all-start.7
  687.6 10.2 %copy.818 = bf16[2,6,10240]{1,0,2:T(2,128)(2,1)} copy(bf16[2,6,10240]{2,0,1:T(2,128)(2,1)} %get-tuple-element.5) | data formatting | bytes 491520 | tf_op jit(solution)/shard_map/convert_element_type | solution.py:92
  697.8 9.9 %reshape.1701 = bf16[4,2,15360]{2,1,0:T(2,128)(2,1)} reshape(bf16[10240,2,6]{2,1,0:T(2,128)(2,1)} %bitcast.1170) | data formatting | bytes 491520
  712.9 8.1 copy.735
  721.1 9.9 %reshape.1693 = bf16[4,2,15360]{2,1,0:T(2,128)(2,1)} reshape(bf16[10240,2,6]{2,1,0:T(2,128)(2,1)} %bitcast.1178) | data formatting | bytes 491520
  735.9 12.6 %reshape.1702 = bf16[10240,2,6]{2,1,0:T(2,128)(2,1)} reshape(bf16[4,2,15360]{2,1,0:T(2,128)(2,1)S(1)} %all-to-all-done.13) | data formatting | bytes 491520
  748.5 12.2 %copy.905 = bf16[2,6,4,2560]{3,2,0,1:T(4,128)(2,1)S(1)} copy(bf16[2,6,4,2560]{1,0,3,2:T(2,128)(2,1)} %bitcast.1171) | data formatting | bytes 491520 | tf_op jit(solution)/shard_map/all_to_all | solution.py:96
  762.1 12.6 %reshape.1694 = bf16[10240,2,6]{2,1,0:T(2,128)(2,1)} reshape(bf16[4,2,15360]{2,1,0:T(2,128)(2,1)S(1)} %all-to-all-done.8) | data formatting | bytes 491520
  774.7 10.2 %copy.736 = bf16[2,6,4,2560]{3,0,2,1:T(2,128)(2,1)S(1)} copy(bf16[2,6,4,2560]{1,0,3,2:T(2,128)(2,1)} %bitcast.1172) | data formatting | bytes 491520 | tf_op jit(solution)/shard_map/all_to_all | solution.py:95
  788.7 4.3 all-to-all-start.9
  841.1 10.3 %copy.821 = bf16[2,6,10240]{1,0,2:T(2,128)(2,1)} copy(bf16[2,6,10240]{2,0,1:T(2,128)(2,1)} %get-tuple-element.3) | data formatting | bytes 491520 | tf_op jit(solution)/shard_map/convert_element_type | solution.py:92
  851.4 9.9 %reshape.1703 = bf16[4,2,15360]{2,1,0:T(2,128)(2,1)} reshape(bf16[10240,2,6]{2,1,0:T(2,128)(2,1)} %bitcast.1173) | data formatting | bytes 491520
  870.4 12.6 %reshape.1704 = bf16[10240,2,6]{2,1,0:T(2,128)(2,1)} reshape(bf16[4,2,15360]{2,1,0:T(2,128)(2,1)S(1)} %all-to-all-done.14) | data formatting | bytes 491520
  883.2 12.3 %copy.906 = bf16[2,6,4,2560]{3,2,0,1:T(4,128)(2,1)S(1)} copy(bf16[2,6,4,2560]{1,0,3,2:T(2,128)(2,1)} %bitcast.1174) | data formatting | bytes 491520 | tf_op jit(solution)/shard_map/all_to_all | solution.py:96
  897.0 23.7 %psum.15 = f32[1,3,64,64]{3,2,1,0:T(8,128)} all-reduce(f32[1,3,64,64]{3,2,1,0:T(8,128)S(1)} %fusion.170), channel_id=1, replica_groups=mesh['section'=4,'tm'=4,'batch'=2] {'tm','batch'}, use_global_device_ids=true, to_apply=%region_1.2 | all-reduce | flops 12288 | bytes 98304 | tf_op jit(solution)/shard_map/psum | solution.py:134
  (812 shorter events, 426.2 us)
Async XLA Ops:
  26.5 99.9 %all-to-all-start = ((bf16[4,2,15360]{2,1,0:T(2,128)(2,1)}), bf16[4,2,15360]{2,1,0:T(2,128)(2,1)}, u32[]{:S(2)}, u32[]{:S(2)}) async-start(bf16[4,2,15360]{2,1,0:T(2,128)(2,1)} %reshape.1685), calls=%async_computation | async-start | bytes 491520 | tf_op jit(solution)/shard_map/all_to_all | solution.py:95
  33.8 160.6 %copy-start.16 = (bf16[128,128,1,1]{1,0,2,3:T(8,128)(2,1)}, bf16[128,128,1,1]{1,0,2,3:T(8,128)(2,1)S(1)}, u32[]{:S(2)}) copy-start(bf16[128,128,1,1]{1,0,2,3:T(8,128)(2,1)S(1)} %reshape.1603) | copy-start | bytes 98308
  33.9 160.8 %copy-start.11 = (bf16[128,128,1,1]{1,0,2,3:T(8,128)(2,1)}, bf16[128,128,1,1]{1,0,2,3:T(8,128)(2,1)S(1)}, u32[]{:S(2)}) copy-start(bf16[128,128,1,1]{1,0,2,3:T(8,128)(2,1)S(1)} %reshape.1604) | copy-start | bytes 98308
  34.1 160.9 %copy-start.6 = (bf16[128,128,1,1]{1,0,2,3:T(8,128)(2,1)}, bf16[128,128,1,1]{1,0,2,3:T(8,128)(2,1)S(1)}, u32[]{:S(2)}) copy-start(bf16[128,128,1,1]{1,0,2,3:T(8,128)(2,1)S(1)} %reshape.1605) | copy-start | bytes 98308
  34.2 162.0 %copy-start.1 = (bf16[128,128,1,1]{1,0,2,3:T(8,128)(2,1)}, bf16[128,128,1,1]{1,0,2,3:T(8,128)(2,1)S(1)}, u32[]{:S(2)}) copy-start(bf16[128,128,1,1]{1,0,2,3:T(8,128)(2,1)S(1)} %reshape.1606) | copy-start | bytes 98308
  34.6 159.6 %copy-start.21 = (bf16[128,128,1,1]{1,0,2,3:T(8,128)(2,1)}, bf16[128,128,1,1]{1,0,2,3:T(8,128)(2,1)S(1)}, u32[]{:S(2)}) copy-start(bf16[128,128,1,1]{1,0,2,3:T(8,128)(2,1)S(1)} %reshape.1602) | copy-start | bytes 98308
  35.7 90.1 %copy-start.43 = (bf16[2,6,80,128]{3,2,0,1:T(8,128)(2,1)}, bf16[2,6,80,128]{3,2,0,1:T(8,128)(2,1)S(1)}, u32[]{:S(2)}) copy-start(bf16[2,6,80,128]{3,2,0,1:T(8,128)(2,1)S(1)} %reshape.1505) | copy-start | bytes 737284
  153.7 9.9 %all-to-all-start.1 = ((bf16[8,6,2560]{2,1,0:T(8,128)(2,1)}), bf16[8,6,2560]{2,1,0:T(8,128)(2,1)S(1)}, u32[]{:S(2)}, u32[]{:S(2)}) async-start(bf16[8,6,2560]{2,1,0:T(8,128)(2,1)} %reshape.1671), calls=%async_computation.1 | async-start | bytes 655360 | tf_op jit(solution)/shard_map/all_to_all | solution.py:100
  202.7 31.0 %collective-permute-start = (bf16[2,6,10240]{2,0,1:T(2,128)(2,1)S(1)}, bf16[2,6,10240]{2,0,1:T(2,128)(2,1)S(1)}, u32[]{:S(2)}, u32[]{:S(2)}) collective-permute-start(bf16[2,6,10240]{2,0,1:T(2,128)(2,1)S(1)} %add_convert_fusion.5), channel_id=1, source_target_pairs={{8,0},{16,8},{24,16},{9,1},{17,9},{25,17},{10,2},{18,10},{26,18},{... | collective-permute-start | bytes 737288 | tf_op jit(solution)/shard_map/ppermute | solution.py:12
  205.1 25.1 %copy-start.162 = (f32[128,128]{1,0:T(8,128)S(1)}, f32[128,128]{1,0:T(8,128)}, u32[]{:S(2)}) copy-start(f32[128,128]{1,0:T(8,128)} %convolution_bitcast_fusion.41) | copy-start | bytes 196612
  205.1 25.7 %copy-start.158 = (f32[128,128]{1,0:T(8,128)S(1)}, f32[128,128]{1,0:T(8,128)}, u32[]{:S(2)}) copy-start(f32[128,128]{1,0:T(8,128)} %convolution_bitcast_fusion.40) | copy-start | bytes 196612
  205.1 26.4 %copy-start.154 = (f32[128,128]{1,0:T(8,128)S(1)}, f32[128,128]{1,0:T(8,128)}, u32[]{:S(2)}) copy-start(f32[128,128]{1,0:T(8,128)} %convolution_bitcast_fusion.39) | copy-start | bytes 196612
  205.1 27.1 %copy-start.150 = (f32[128,128]{1,0:T(8,128)S(1)}, f32[128,128]{1,0:T(8,128)}, u32[]{:S(2)}) copy-start(f32[128,128]{1,0:T(8,128)} %convolution_bitcast_fusion.38) | copy-start | bytes 196612
  205.1 27.8 %copy-start.149 = (f32[128,128]{1,0:T(8,128)S(1)}, f32[128,128]{1,0:T(8,128)}, u32[]{:S(2)}) copy-start(f32[128,128]{1,0:T(8,128)} %convolution_bitcast_fusion.37) | copy-start | bytes 196612
  225.4 26.6 %all-to-all-start.10 = ((bf16[4,2,15360]{2,1,0:T(2,128)(2,1)}), bf16[4,2,15360]{2,1,0:T(2,128)(2,1)S(1)}, u32[]{:S(2)}, u32[]{:S(2)}) async-start(bf16[4,2,15360]{2,1,0:T(2,128)(2,1)} %reshape.1695), calls=%async_computation.10 | async-start | bytes 491520 | tf_op jit(solution)/shard_map/all_to_all | solution.py:96
  252.0 31.3 %all-to-all-start.2 = ((bf16[4,2,15360]{2,1,0:T(2,128)(2,1)}), bf16[4,2,15360]{2,1,0:T(2,128)(2,1)S(1)}, u32[]{:S(2)}, u32[]{:S(2)}) async-start(bf16[4,2,15360]{2,1,0:T(2,128)(2,1)} %reshape.1687), calls=%async_computation.2 | async-start | bytes 491520 | tf_op jit(solution)/shard_map/all_to_all | solution.py:95
  314.8 10.0 %all-to-all-start.3 = ((bf16[8,6,2560]{2,1,0:T(8,128)(2,1)}), bf16[8,6,2560]{2,1,0:T(8,128)(2,1)}, u32[]{:S(2)}, u32[]{:S(2)}) async-start(bf16[8,6,2560]{2,1,0:T(8,128)(2,1)} %reshape.1681), calls=%async_computation.3 | async-start | bytes 655360 | tf_op jit(solution)/shard_map/all_to_all | solution.py:100
  364.0 31.2 %collective-permute-start.1 = (bf16[2,6,10240]{2,0,1:T(2,128)(2,1)S(1)}, bf16[2,6,10240]{2,0,1:T(2,128)(2,1)S(1)}, u32[]{:S(2)}, u32[]{:S(2)}) collective-permute-start(bf16[2,6,10240]{2,0,1:T(2,128)(2,1)S(1)} %add_convert_fusion.4), channel_id=1, source_target_pairs={{8,0},{16,8},{24,16},{9,1},{17,9},{25,17},{10,2},{18,10},{26,18},{... | collective-permute-start | bytes 737288 | tf_op jit(solution)/shard_map/ppermute | solution.py:12
  366.4 25.4 %copy-start.167 = (f32[128,128]{1,0:T(8,128)S(1)}, f32[128,128]{1,0:T(8,128)}, u32[]{:S(2)}) copy-start(f32[128,128]{1,0:T(8,128)} %convolution_bitcast_fusion.32) | copy-start | bytes 196612
  366.4 26.1 %copy-start.163 = (f32[128,128]{1,0:T(8,128)S(1)}, f32[128,128]{1,0:T(8,128)}, u32[]{:S(2)}) copy-start(f32[128,128]{1,0:T(8,128)} %convolution_bitcast_fusion.31) | copy-start | bytes 196612
  366.4 26.8 %copy-start.159 = (f32[128,128]{1,0:T(8,128)S(1)}, f32[128,128]{1,0:T(8,128)}, u32[]{:S(2)}) copy-start(f32[128,128]{1,0:T(8,128)} %convolution_bitcast_fusion.30) | copy-start | bytes 196612
  366.4 27.4 %copy-start.155 = (f32[128,128]{1,0:T(8,128)S(1)}, f32[128,128]{1,0:T(8,128)}, u32[]{:S(2)}) copy-start(f32[128,128]{1,0:T(8,128)} %convolution_bitcast_fusion.29) | copy-start | bytes 196612
  366.4 28.1 %copy-start.151 = (f32[128,128]{1,0:T(8,128)S(1)}, f32[128,128]{1,0:T(8,128)}, u32[]{:S(2)}) copy-start(f32[128,128]{1,0:T(8,128)} %convolution_bitcast_fusion.28) | copy-start | bytes 196612
  386.6 26.9 %all-to-all-start.11 = ((bf16[4,2,15360]{2,1,0:T(2,128)(2,1)}), bf16[4,2,15360]{2,1,0:T(2,128)(2,1)S(1)}, u32[]{:S(2)}, u32[]{:S(2)}) async-start(bf16[4,2,15360]{2,1,0:T(2,128)(2,1)} %reshape.1697), calls=%async_computation.11 | async-start | bytes 491520 | tf_op jit(solution)/shard_map/all_to_all | solution.py:96
  413.6 31.1 %all-to-all-start.4 = ((bf16[4,2,15360]{2,1,0:T(2,128)(2,1)}), bf16[4,2,15360]{2,1,0:T(2,128)(2,1)S(1)}, u32[]{:S(2)}, u32[]{:S(2)}) async-start(bf16[4,2,15360]{2,1,0:T(2,128)(2,1)} %reshape.1689), calls=%async_computation.4 | async-start | bytes 491520 | tf_op jit(solution)/shard_map/all_to_all | solution.py:95
  476.2 10.0 %all-to-all-start.5 = ((bf16[8,6,2560]{2,1,0:T(8,128)(2,1)}), bf16[8,6,2560]{2,1,0:T(8,128)(2,1)}, u32[]{:S(2)}, u32[]{:S(2)}) async-start(bf16[8,6,2560]{2,1,0:T(8,128)(2,1)} %reshape.1682), calls=%async_computation.5 | async-start | bytes 655360 | tf_op jit(solution)/shard_map/all_to_all | solution.py:100
  523.5 30.9 %collective-permute-start.2 = (bf16[2,6,10240]{2,0,1:T(2,128)(2,1)S(1)}, bf16[2,6,10240]{2,0,1:T(2,128)(2,1)S(1)}, u32[]{:S(2)}, u32[]{:S(2)}) collective-permute-start(bf16[2,6,10240]{2,0,1:T(2,128)(2,1)S(1)} %add_convert_fusion.3), channel_id=1, source_target_pairs={{8,0},{16,8},{24,16},{9,1},{17,9},{25,17},{10,2},{18,10},{26,18},{... | collective-permute-start | bytes 737288 | tf_op jit(solution)/shard_map/ppermute | solution.py:12
  525.7 25.2 %copy-start.169 = (f32[128,128]{1,0:T(8,128)S(1)}, f32[128,128]{1,0:T(8,128)}, u32[]{:S(2)}) copy-start(f32[128,128]{1,0:T(8,128)} %convolution_bitcast_fusion.23) | copy-start | bytes 196612
  525.7 25.9 %copy-start.165 = (f32[128,128]{1,0:T(8,128)S(1)}, f32[128,128]{1,0:T(8,128)}, u32[]{:S(2)}) copy-start(f32[128,128]{1,0:T(8,128)} %convolution_bitcast_fusion.22) | copy-start | bytes 196612
  525.7 26.6 %copy-start.161 = (f32[128,128]{1,0:T(8,128)S(1)}, f32[128,128]{1,0:T(8,128)}, u32[]{:S(2)}) copy-start(f32[128,128]{1,0:T(8,128)} %convolution_bitcast_fusion.21) | copy-start | bytes 196612
  525.7 27.2 %copy-start.157 = (f32[128,128]{1,0:T(8,128)S(1)}, f32[128,128]{1,0:T(8,128)}, u32[]{:S(2)}) copy-start(f32[128,128]{1,0:T(8,128)} %convolution_bitcast_fusion.20) | copy-start | bytes 196612
  525.7 27.9 %copy-start.153 = (f32[128,128]{1,0:T(8,128)S(1)}, f32[128,128]{1,0:T(8,128)}, u32[]{:S(2)}) copy-start(f32[128,128]{1,0:T(8,128)} %convolution_bitcast_fusion.19) | copy-start | bytes 196612
  545.9 26.8 %all-to-all-start.12 = ((bf16[4,2,15360]{2,1,0:T(2,128)(2,1)}), bf16[4,2,15360]{2,1,0:T(2,128)(2,1)S(1)}, u32[]{:S(2)}, u32[]{:S(2)}) async-start(bf16[4,2,15360]{2,1,0:T(2,128)(2,1)} %reshape.1699), calls=%async_computation.12 | async-start | bytes 491520 | tf_op jit(solution)/shard_map/all_to_all | solution.py:96
  572.7 31.3 %all-to-all-start.6 = ((bf16[4,2,15360]{2,1,0:T(2,128)(2,1)}), bf16[4,2,15360]{2,1,0:T(2,128)(2,1)S(1)}, u32[]{:S(2)}, u32[]{:S(2)}) async-start(bf16[4,2,15360]{2,1,0:T(2,128)(2,1)} %reshape.1691), calls=%async_computation.6 | async-start | bytes 491520 | tf_op jit(solution)/shard_map/all_to_all | solution.py:95
  635.5 10.2 %all-to-all-start.7 = ((bf16[8,6,2560]{2,1,0:T(8,128)(2,1)}), bf16[8,6,2560]{2,1,0:T(8,128)(2,1)}, u32[]{:S(2)}, u32[]{:S(2)}) async-start(bf16[8,6,2560]{2,1,0:T(8,128)(2,1)} %reshape.1683), calls=%async_computation.7 | async-start | bytes 655360 | tf_op jit(solution)/shard_map/all_to_all | solution.py:100
  685.6 27.1 %collective-permute-start.3 = (bf16[2,6,10240]{2,0,1:T(2,128)(2,1)S(1)}, bf16[2,6,10240]{2,0,1:T(2,128)(2,1)S(1)}, u32[]{:S(2)}, u32[]{:S(2)}) collective-permute-start(bf16[2,6,10240]{2,0,1:T(2,128)(2,1)S(1)} %add_convert_fusion.2), channel_id=1, source_target_pairs={{8,0},{16,8},{24,16},{9,1},{17,9},{25,17},{10,2},{18,10},{26,18},{... | collective-permute-start | bytes 737288 | tf_op jit(solution)/shard_map/ppermute | solution.py:12
  687.5 24.6 %copy-start.171 = (f32[128,128]{1,0:T(8,128)S(1)}, f32[128,128]{1,0:T(8,128)}, u32[]{:S(2)}) copy-start(f32[128,128]{1,0:T(8,128)} %convolution_bitcast_fusion.15) | copy-start | bytes 196612
  687.5 24.7 %copy-start.168 = (f32[128,128]{1,0:T(8,128)S(1)}, f32[128,128]{1,0:T(8,128)}, u32[]{:S(2)}) copy-start(f32[128,128]{1,0:T(8,128)} %convolution_bitcast_fusion.14) | copy-start | bytes 196612
  687.5 24.7 %copy-start.164 = (f32[128,128]{1,0:T(8,128)S(1)}, f32[128,128]{1,0:T(8,128)}, u32[]{:S(2)}) copy-start(f32[128,128]{1,0:T(8,128)} %convolution_bitcast_fusion.13) | copy-start | bytes 196612
  687.6 24.8 %copy-start.160 = (f32[128,128]{1,0:T(8,128)S(1)}, f32[128,128]{1,0:T(8,128)}, u32[]{:S(2)}) copy-start(f32[128,128]{1,0:T(8,128)} %convolution_bitcast_fusion.12) | copy-start | bytes 196612
  687.6 24.9 %copy-start.156 = (f32[128,128]{1,0:T(8,128)S(1)}, f32[128,128]{1,0:T(8,128)}, u32[]{:S(2)}) copy-start(f32[128,128]{1,0:T(8,128)} %convolution_bitcast_fusion.11) | copy-start | bytes 196612
  687.6 25.0 %copy-start.152 = (f32[128,128]{1,0:T(8,128)S(1)}, f32[128,128]{1,0:T(8,128)}, u32[]{:S(2)}) copy-start(f32[128,128]{1,0:T(8,128)} %convolution_bitcast_fusion.10) | copy-start | bytes 196612
  707.7 23.3 %all-to-all-start.13 = ((bf16[4,2,15360]{2,1,0:T(2,128)(2,1)}), bf16[4,2,15360]{2,1,0:T(2,128)(2,1)S(1)}, u32[]{:S(2)}, u32[]{:S(2)}) async-start(bf16[4,2,15360]{2,1,0:T(2,128)(2,1)} %reshape.1701), calls=%async_computation.13 | async-start | bytes 491520 | tf_op jit(solution)/shard_map/all_to_all | solution.py:96
  731.0 31.1 %all-to-all-start.8 = ((bf16[4,2,15360]{2,1,0:T(2,128)(2,1)}), bf16[4,2,15360]{2,1,0:T(2,128)(2,1)S(1)}, u32[]{:S(2)}, u32[]{:S(2)}) async-start(bf16[4,2,15360]{2,1,0:T(2,128)(2,1)} %reshape.1693), calls=%async_computation.8 | async-start | bytes 491520 | tf_op jit(solution)/shard_map/all_to_all | solution.py:95
  735.9 24.8 %copy-start.122 = (f32[9,64,64]{2,1,0:T(8,128)}, f32[9,64,64]{2,1,0:T(8,128)S(1)}, u32[]{:S(2)}) copy-start(f32[9,64,64]{2,1,0:T(8,128)S(1)} %get-tuple-element.143) | copy-start | bytes 442372
  788.7 9.9 %all-to-all-start.9 = ((bf16[8,6,2560]{2,1,0:T(8,128)(2,1)}), bf16[8,6,2560]{2,1,0:T(8,128)(2,1)S(1)}, u32[]{:S(2)}, u32[]{:S(2)}) async-start(bf16[8,6,2560]{2,1,0:T(8,128)(2,1)} %reshape.1684), calls=%async_computation.9 | async-start | bytes 655360 | tf_op jit(solution)/shard_map/all_to_all | solution.py:100
  793.0 127.7 %all-reduce.17.cloned.1.call-start = ((), (), s32[]{:S(2)}) async-start(), calls=%async_computation.15 | async-start | bytes 589824 | tf_op jit(solution)/shard_map/psum | solution.py:134
  861.3 9.1 all-to-all-start.14
  (151 other events, 1933.2 us)
Sparse Core Ops, SparseCore 0:
  820.6 53.1 all-reduce.16
where the time goes:
time: 944 us; the launch traced here: 930 us
  local copies, waits for them, and re-layouts  609 us (65%)
  matrix products  137 us (15%)
  starting transfers between devices  70 us (7%)
  other arithmetic  49 us (5%)
  blocking collectives  23.7 us (3%)
  waiting for transfers between devices  23.2 us (2%)
  between operations  17.9 us (2%)
    unnamed x379, local copies, waits for them, and re-layouts  229 us
    reshape x105, local copies, waits for them, and re-layouts, split_pixels(): return a.reshape(a.shape[:-1] + (a.shape[-1] // chans, chans))  112 us
    all_to_all x10, local copies, waits for them, and re-layouts, section_backward(): lax.all_to_all(h, 'tm', split_axis=2, concat_axis=0, tiled=True)  61.8 us
    dot_general x45, matrix products, spatial_back(): jnp.einsum('nrpa,nrpb->ab', xpiece, gz_pairs, preferred_element_type=jnp....  54.5 us
    all_to_all x10, local copies, waits for them, and re-layouts, section_backward(): lax.all_to_all(gradient_piece, 'tm', split_axis=2, concat_axis=0, tiled=T...  52.1 us
    convert_element_type x5, local copies, waits for them, and re-layouts, section_backward(): h = (z * sig).astype(jnp.bfloat16)  51.3 us
    select_n x5, local copies, waits for them, and re-layouts, body(): incoming = jnp.where(section_idx == number_sections - 1, top_grad, received)  40.8 us
    dot_general x45, matrix products, spatial_fwd(): jnp.einsum('nrpa,ab->nrpb', piece, paired_kernel(ws[3 * i + j]), preferre...  28.6 us
  transfers between devices with their start and end apart: 20, of which 6 were waited for; matrix products, arithmetic and copies ran while one was open for 48% of the time, Pallas kernels for 0%

commit v1 on v0

--- a/solution.py
+++ b/solution.py
@@ -4,6 +4,15 @@
 from jax.sharding import PartitionSpec as P
 
 TIME_DILATION = 2
+_store_bench = lambda local_values, comm_axis: jnp.concatenate(
+    lax.all_to_all(
+        jnp.stack(jnp.split(local_values, lax.axis_size(comm_axis), 2), axis=0),
+        axis_name=comm_axis,
+        split_axis=0,
+        concat_axis=0,
+    ),
+    0,
+)
 
 
 def from_behind(value, axis, steps):
@@ -93,7 +102,7 @@
     deriv = sig * (1.0 + z * (1.0 - sig))
     tile_gradient, h_tile = (
         lax.all_to_all(gradient_piece, "tm", split_axis=2, concat_axis=0, tiled=True),
-        lax.all_to_all(h, "tm", split_axis=2, concat_axis=0, tiled=True),
+        _store_bench(h, "tm"),
     )
     gradient_padded = jnp.pad(tile_gradient, ((dilation_step, dilation_step), (0, 0), (0, 0)))
     gh_tile, tgrads = temporal_back(h_tile, tile_gradient, gradient_padded, dilation_step, wt)

time: 944 us -> 768 us (0.81)
  local copies, waits for them, and re-layouts: 609 us -> 390 us
  other arithmetic: 49 us -> 74.8 us
  waiting for transfers between devices: 23.2 us -> 37.3 us
    unnamed x379 -> x285, local copies, waits for them, and re-layouts: 229 us -> 117 us
    all_to_all x10 -> x5, local copies, waits for them, and re-layouts: 61.8 us -> 4.63 us  [lax.all_to_all(jnp.stack(jnp.split(local_values, lax.axis_size(comm_axis)...]
    convert_element_type x5 -> x0, local copies, waits for them, and re-layouts: 51.3 us -> none  [section_backward(): h = (z * sig).astype(jnp.bfloat16)]
    unnamed x40, other arithmetic: 24.6 us -> 45.6 us
    all_to_all x5, waiting for transfers between devices: 0.01 us -> 9.65 us  [section_backward(): lax.all_to_all(gradient_piece, 'tm', split_axis=2, concat_axis=0, tiled=T...]
    reshape x105 -> x100, local copies, waits for them, and re-layouts: 112 us -> 109 us  [split_pixels(): return a.reshape(a.shape[:-1] + (a.shape[-1] // chans, chans))]
  transfers between devices with their start and end apart: 20 -> 20, of which waited for: 6 -> 10; matrix products, arithmetic and copies ran while one was open for 48% -> 42% of each run, Pallas kernels for 0% -> 0%
where the time goes in v1:
time: 768 us; the launch traced here: 755 us
  local copies, waits for them, and re-layouts  390 us (51%)
  matrix products  140 us (18%)
  other arithmetic  74.8 us (10%)
  starting transfers between devices  71.3 us (9%)
  waiting for transfers between devices  37.3 us (5%)
  blocking collectives  24 us (3%)
  between operations  17.4 us (2%)
    unnamed x285, local copies, waits for them, and re-layouts  117 us
    reshape x100, local copies, waits for them, and re-layouts, split_pixels(): return a.reshape(a.shape[:-1] + (a.shape[-1] // chans, chans))  109 us
    dot_general x45, matrix products, spatial_back(): jnp.einsum('nrpa,nrpb->ab', xpiece, gz_pairs, preferred_element_type=jnp....  59 us
    all_to_all x10, local copies, waits for them, and re-layouts, section_backward(): lax.all_to_all(gradient_piece, 'tm', split_axis=2, concat_axis=0, tiled=T...  51.7 us
    unnamed x40, other arithmetic  45.6 us
    select_n x5, local copies, waits for them, and re-layouts, body(): incoming = jnp.where(section_idx == number_sections - 1, top_grad, received)  40.7 us
    dot_general x45, matrix products, spatial_fwd(): jnp.einsum('nrpa,ab->nrpb', piece, paired_kernel(ws[3 * i + j]), preferre...  28.6 us
    dot_general x45, matrix products, spatial_back(): jnp.einsum('nrpb,ab->nrpa', gpiece, paired_kernel(ws[3 * i + j]), preferr...  27.4 us
  transfers between devices with their start and end apart: 20, of which 10 were waited for; matrix products, arithmetic and copies ran while one was open for 42% of the time, Pallas kernels for 0%

profile of v1, /device:TPU:24, one launch (start us, length us, event | category | flops | bytes accessed | tf_op | source)
XLA Modules:
  0.0 754.8 jit_solution(11102432508037530175)
XLA Ops:
  8.3 8.1 %copy.603 = bf16[2,6,10240]{1,0,2:T(2,128)(2,1)} copy(bf16[2,6,10240]{2,0,1:T(2,128)(2,1)S(1)} %fusion.321) | data formatting | bytes 491520 | tf_op jit(solution)/shard_map/jit(_where)/select_n | solution.py:134
  16.5 10.0 %reshape.1660 = bf16[4,2,15360]{2,1,0:T(2,128)(2,1)} reshape(bf16[10240,2,6]{2,1,0:T(2,128)(2,1)} %bitcast.1179) | data formatting | bytes 491520
  26.4 4.6 all-to-all-start
  49.3 3.0 pad_slice_fusion.82
  60.8 3.0 pad_slice_fusion.66
  75.0 3.2 pad_slice_fusion.50
  90.2 3.1 pad_slice_fusion.18
  125.6 13.6 %reshape.1661 = bf16[10240,2,6]{2,1,0:T(2,128)(2,1)} reshape(bf16[4,2,15360]{2,1,0:T(2,128)(2,1)} %all-to-all-done) | data formatting | bytes 491520
  139.2 10.2 %copy.604 = bf16[2,6,4,2560]{3,0,2,1:T(2,128)(2,1)S(1)} copy(bf16[2,6,4,2560]{1,0,3,2:T(2,128)(2,1)} %bitcast.1180) | data formatting | bytes 491520 | tf_op jit(solution)/shard_map/all_to_all | solution.py:104
  152.5 4.7 all-to-all-start.1
  158.3 4.5 all-to-all-done.1
  199.6 3.4 all-to-all-start.10
  215.1 8.1 %copy.631 = bf16[2,6,10240]{1,0,2:T(2,128)(2,1)} copy(bf16[2,6,10240]{2,0,1:T(2,128)(2,1)S(1)} %broadcast_select_fusion.9) | data formatting | bytes 491520 | tf_op jit(solution)/shard_map/jit(_where)/select_n | solution.py:134
  223.3 9.9 %reshape.1662 = bf16[4,2,15360]{2,1,0:T(2,128)(2,1)} reshape(bf16[10240,2,6]{2,1,0:T(2,128)(2,1)} %bitcast.1185) | data formatting | bytes 491520
  233.2 4.2 all-to-all-start.2
  239.6 3.0 all-to-all-done.2
  242.7 12.6 %reshape.1663 = bf16[10240,2,6]{2,1,0:T(2,128)(2,1)} reshape(bf16[4,2,15360]{2,1,0:T(2,128)(2,1)S(1)} %all-to-all-done.2) | data formatting | bytes 491520
  255.3 10.2 %copy.632 = bf16[2,6,4,2560]{3,0,2,1:T(2,128)(2,1)S(1)} copy(bf16[2,6,4,2560]{1,0,3,2:T(2,128)(2,1)} %bitcast.1181) | data formatting | bytes 491520 | tf_op jit(solution)/shard_map/all_to_all | solution.py:104
  274.2 4.3 all-to-all-start.3
  280.3 3.8 all-to-all-done.3
  304.6 4.0 all-to-all-start.11
  341.9 8.1 %copy.659 = bf16[2,6,10240]{1,0,2:T(2,128)(2,1)} copy(bf16[2,6,10240]{2,0,1:T(2,128)(2,1)S(1)} %broadcast_select_fusion.8) | data formatting | bytes 491520 | tf_op jit(solution)/shard_map/jit(_where)/select_n | solution.py:134
  350.1 9.9 %reshape.1664 = bf16[4,2,15360]{2,1,0:T(2,128)(2,1)} reshape(bf16[10240,2,6]{2,1,0:T(2,128)(2,1)} %bitcast.1186) | data formatting | bytes 491520
  360.0 4.1 all-to-all-start.4
  369.5 12.6 %reshape.1665 = bf16[10240,2,6]{2,1,0:T(2,128)(2,1)} reshape(bf16[4,2,15360]{2,1,0:T(2,128)(2,1)S(1)} %all-to-all-done.4) | data formatting | bytes 491520
  382.1 10.2 %copy.660 = bf16[2,6,4,2560]{3,0,2,1:T(2,128)(2,1)S(1)} copy(bf16[2,6,4,2560]{1,0,3,2:T(2,128)(2,1)} %bitcast.1182) | data formatting | bytes 491520 | tf_op jit(solution)/shard_map/all_to_all | solution.py:104
  401.0 4.1 all-to-all-start.5
  406.9 3.8 all-to-all-done.5
  429.4 4.4 all-to-all-start.12
  468.9 8.1 %copy.687 = bf16[2,6,10240]{1,0,2:T(2,128)(2,1)} copy(bf16[2,6,10240]{2,0,1:T(2,128)(2,1)S(1)} %broadcast_select_fusion.7) | data formatting | bytes 491520 | tf_op jit(solution)/shard_map/jit(_where)/select_n | solution.py:134
  477.0 9.9 %reshape.1666 = bf16[4,2,15360]{2,1,0:T(2,128)(2,1)} reshape(bf16[10240,2,6]{2,1,0:T(2,128)(2,1)} %bitcast.1187) | data formatting | bytes 491520
  486.9 4.2 all-to-all-start.6
  496.4 12.6 %reshape.1667 = bf16[10240,2,6]{2,1,0:T(2,128)(2,1)} reshape(bf16[4,2,15360]{2,1,0:T(2,128)(2,1)S(1)} %all-to-all-done.6) | data formatting | bytes 491520
  509.0 10.2 %copy.688 = bf16[2,6,4,2560]{3,0,2,1:T(2,128)(2,1)S(1)} copy(bf16[2,6,4,2560]{1,0,3,2:T(2,128)(2,1)} %bitcast.1183) | data formatting | bytes 491520 | tf_op jit(solution)/shard_map/all_to_all | solution.py:104
  527.9 4.3 all-to-all-start.7
  534.0 3.8 all-to-all-done.7
  558.3 4.0 all-to-all-start.13
  595.2 8.1 %copy.715 = bf16[2,6,10240]{1,0,2:T(2,128)(2,1)} copy(bf16[2,6,10240]{2,0,1:T(2,128)(2,1)S(1)} %broadcast_select_fusion.6) | data formatting | bytes 491520 | tf_op jit(solution)/shard_map/jit(_where)/select_n | solution.py:134
  603.4 9.9 %reshape.1668 = bf16[4,2,15360]{2,1,0:T(2,128)(2,1)} reshape(bf16[10240,2,6]{2,1,0:T(2,128)(2,1)} %bitcast.1188) | data formatting | bytes 491520
  613.3 4.2 all-to-all-start.8
  622.8 12.6 %reshape.1669 = bf16[10240,2,6]{2,1,0:T(2,128)(2,1)} reshape(bf16[4,2,15360]{2,1,0:T(2,128)(2,1)S(1)} %all-to-all-done.8) | data formatting | bytes 491520
  635.4 10.2 %copy.716 = bf16[2,6,4,2560]{3,0,2,1:T(2,128)(2,1)S(1)} copy(bf16[2,6,4,2560]{1,0,3,2:T(2,128)(2,1)} %bitcast.1184) | data formatting | bytes 491520 | tf_op jit(solution)/shard_map/all_to_all | solution.py:104
  649.4 3.6 all-to-all-start.9
  654.8 3.7 all-to-all-done.9
  677.1 4.2 all-to-all-start.14
  707.6 3.1 broadcast_select_fusion.3
  714.0 24.0 %psum.15 = f32[1,3,64,64]{3,2,1,0:T(8,128)} all-reduce(f32[1,3,64,64]{3,2,1,0:T(8,128)S(1)} %fusion.170), channel_id=1, replica_groups=mesh['section'=4,'tm'=4,'batch'=2] {'tm','batch'}, use_global_device_ids=true, to_apply=%region_1.2 | all-reduce | flops 12288 | bytes 98304 | tf_op jit(solution)/shard_map/psum | solution.py:143
  738.0 8.0 %all-reduce.17.cloned.1.call-done = f32[1,9,64,64]{3,2,1,0:T(8,128)} async-done(((f32[1,9,64,64]{3,2,1,0:T(8,128)}), f32[1,9,64,64]{3,2,1,0:T(8,128)}) %all-reduce.17.cloned.1.call-update) | async-done | bytes 147472 | tf_op jit(solution)/shard_map/psum | solution.py:143
  (718 shorter events, 399.6 us)
Async XLA Ops:
  8.3 23.3 %copy-start.125 = (bf16[1,9,64,64]{3,2,1,0:T(8,128)(2,1)S(1)}, bf16[1,9,64,64]{3,2,1,0:T(8,128)(2,1)}, u32[]{:S(2)}) copy-start(bf16[1,9,64,64]{3,2,1,0:T(8,128)(2,1)} %param.6) | copy-start | bytes 221188
  26.4 99.2 %all-to-all-start = ((bf16[4,2,15360]{2,1,0:T(2,128)(2,1)}), bf16[4,2,15360]{2,1,0:T(2,128)(2,1)}, u32[]{:S(2)}, u32[]{:S(2)}) async-start(bf16[4,2,15360]{2,1,0:T(2,128)(2,1)} %reshape.1660), calls=%async_computation | async-start | bytes 491520 | tf_op jit(solution)/shard_map/all_to_all | solution.py:104
  33.0 158.8 %copy-start.16 = (bf16[128,128,1,1]{1,0,2,3:T(8,128)(2,1)}, bf16[128,128,1,1]{1,0,2,3:T(8,128)(2,1)S(1)}, u32[]{:S(2)}) copy-start(bf16[128,128,1,1]{1,0,2,3:T(8,128)(2,1)S(1)} %reshape.1578) | copy-start | bytes 98308
  33.1 160.0 %copy-start.11 = (bf16[128,128,1,1]{1,0,2,3:T(8,128)(2,1)}, bf16[128,128,1,1]{1,0,2,3:T(8,128)(2,1)S(1)}, u32[]{:S(2)}) copy-start(bf16[128,128,1,1]{1,0,2,3:T(8,128)(2,1)S(1)} %reshape.1579) | copy-start | bytes 98308
  33.2 160.1 %copy-start.6 = (bf16[128,128,1,1]{1,0,2,3:T(8,128)(2,1)}, bf16[128,128,1,1]{1,0,2,3:T(8,128)(2,1)S(1)}, u32[]{:S(2)}) copy-start(bf16[128,128,1,1]{1,0,2,3:T(8,128)(2,1)S(1)} %reshape.1580) | copy-start | bytes 98308
  33.4 160.3 %copy-start.1 = (bf16[128,128,1,1]{1,0,2,3:T(8,128)(2,1)}, bf16[128,128,1,1]{1,0,2,3:T(8,128)(2,1)S(1)}, u32[]{:S(2)}) copy-start(bf16[128,128,1,1]{1,0,2,3:T(8,128)(2,1)S(1)} %reshape.1581) | copy-start | bytes 98308
  33.8 157.8 %copy-start.21 = (bf16[128,128,1,1]{1,0,2,3:T(8,128)(2,1)}, bf16[128,128,1,1]{1,0,2,3:T(8,128)(2,1)S(1)}, u32[]{:S(2)}) copy-start(bf16[128,128,1,1]{1,0,2,3:T(8,128)(2,1)S(1)} %reshape.1577) | copy-start | bytes 98308
  34.9 90.1 %copy-start.42 = (bf16[2,6,80,128]{3,2,0,1:T(8,128)(2,1)}, bf16[2,6,80,128]{3,2,0,1:T(8,128)(2,1)S(1)}, u32[]{:S(2)}) copy-start(bf16[2,6,80,128]{3,2,0,1:T(8,128)(2,1)S(1)} %reshape.1485) | copy-start | bytes 737284
  152.5 10.3 %all-to-all-start.1 = ((bf16[8,6,2560]{2,1,0:T(8,128)(2,1)}), bf16[8,6,2560]{2,1,0:T(8,128)(2,1)S(1)}, u32[]{:S(2)}, u32[]{:S(2)}) async-start(bf16[8,6,2560]{2,1,0:T(8,128)(2,1)} %reshape.1646), calls=%async_computation.1 | async-start | bytes 655360 | tf_op jit(solution)/shard_map/all_to_all | solution.py:109
  199.6 33.6 %all-to-all-start.10 = ((bf16[4,2,6,2560]{3,1,2,0:T(2,128)(2,1)}), bf16[4,2,6,2560]{3,1,2,0:T(2,128)(2,1)S(1)}, u32[]{:S(2)}, u32[]{:S(2)}) async-start(bf16[4,2,6,2560]{3,1,2,0:T(2,128)(2,1)} %pad_maximum_fusion), calls=%async_computation.10 | async-start | bytes 491520 | tf_op jit(solution)/shard_map/all_to_all | solution.py:8
  205.2 9.7 %collective-permute-start = (bf16[2,6,10240]{2,0,1:T(2,128)(2,1)S(1)}, bf16[2,6,10240]{2,0,1:T(2,128)(2,1)S(1)}, u32[]{:S(2)}, u32[]{:S(2)}) collective-permute-start(bf16[2,6,10240]{2,0,1:T(2,128)(2,1)S(1)} %add_convert_fusion.5), channel_id=1, source_target_pairs={{8,0},{16,8},{24,16},{9,1},{17,9},{25,17},{10,2},{18,10},{26,18},{... | collective-permute-start | bytes 737288 | tf_op jit(solution)/shard_map/ppermute | solution.py:21
  215.1 22.2 %copy-start.117 = (bf16[2,6,80,128]{3,2,1,0:T(8,128)(2,1)S(1)}, bf16[2,6,80,128]{3,2,1,0:T(8,128)(2,1)}, u32[]{:S(2)}) copy-start(bf16[2,6,80,128]{3,2,1,0:T(8,128)(2,1)} %copy-done.116) | copy-start | bytes 737284
  215.1 22.2 %copy-start.124 = (bf16[2,6,80,128]{3,2,0,1:T(8,128)(2,1)S(1)}, bf16[2,6,80,128]{3,2,0,1:T(8,128)(2,1)}, u32[]{:S(2)}) copy-start(bf16[2,6,80,128]{3,2,0,1:T(8,128)(2,1)} %reshape.1380) | copy-start | bytes 737284
  233.2 9.5 %all-to-all-start.2 = ((bf16[4,2,15360]{2,1,0:T(2,128)(2,1)}), bf16[4,2,15360]{2,1,0:T(2,128)(2,1)S(1)}, u32[]{:S(2)}, u32[]{:S(2)}) async-start(bf16[4,2,15360]{2,1,0:T(2,128)(2,1)} %reshape.1662), calls=%async_computation.2 | async-start | bytes 491520 | tf_op jit(solution)/shard_map/all_to_all | solution.py:104
  274.2 9.9 %all-to-all-start.3 = ((bf16[8,6,2560]{2,1,0:T(8,128)(2,1)}), bf16[8,6,2560]{2,1,0:T(8,128)(2,1)}, u32[]{:S(2)}, u32[]{:S(2)}) async-start(bf16[8,6,2560]{2,1,0:T(8,128)(2,1)} %reshape.1656), calls=%async_computation.3 | async-start | bytes 655360 | tf_op jit(solution)/shard_map/all_to_all | solution.py:109
  301.0 22.2 %copy-start.22 = (bf16[128,128,1,1]{1,0,2,3:T(8,128)(2,1)S(1)}, bf16[128,128,1,1]{1,0,2,3:T(8,128)(2,1)}, u32[]{:S(2)}) copy-start(bf16[128,128,1,1]{1,0,2,3:T(8,128)(2,1)} %copy-done.21) | copy-start | bytes 98308
  301.0 22.5 %copy-start.17 = (bf16[128,128,1,1]{1,0,2,3:T(8,128)(2,1)S(1)}, bf16[128,128,1,1]{1,0,2,3:T(8,128)(2,1)}, u32[]{:S(2)}) copy-start(bf16[128,128,1,1]{1,0,2,3:T(8,128)(2,1)} %copy-done.16) | copy-start | bytes 98308
  304.6 55.4 %all-to-all-start.11 = ((bf16[4,2,6,2560]{3,1,2,0:T(2,128)(2,1)}), bf16[4,2,6,2560]{3,1,2,0:T(2,128)(2,1)}, u32[]{:S(2)}, u32[]{:S(2)}) async-start(bf16[4,2,6,2560]{3,1,2,0:T(2,128)(2,1)} %pad_maximum_fusion.1), calls=%async_computation.11 | async-start | bytes 491520 | tf_op jit(solution)/shard_map/all_to_all | solution.py:8
  329.8 30.1 %copy-start.103 = (bf16[2,6,10240]{2,0,1:T(2,128)(2,1)}, bf16[2,6,10240]{2,0,1:T(2,128)(2,1)S(1)}, u32[]{:S(2)}) copy-start(bf16[2,6,10240]{2,0,1:T(2,128)(2,1)S(1)} %add_convert_fusion.4) | copy-start | bytes 737284
  329.9 11.8 %collective-permute-start.1 = (bf16[2,6,10240]{2,0,1:T(2,128)(2,1)S(1)}, bf16[2,6,10240]{2,0,1:T(2,128)(2,1)S(1)}, u32[]{:S(2)}, u32[]{:S(2)}) collective-permute-start(bf16[2,6,10240]{2,0,1:T(2,128)(2,1)S(1)} %add_convert_fusion.4), channel_id=1, source_target_pairs={{8,0},{16,8},{24,16},{9,1},{17,9},{25,17},{10,2},{18,10},{26,18},{... | collective-permute-start | bytes 737288 | tf_op jit(solution)/shard_map/ppermute | solution.py:21
  341.9 22.2 %copy-start.130 = (f32[128,128]{1,0:T(8,128)S(1)}, f32[128,128]{1,0:T(8,128)}, u32[]{:S(2)}) copy-start(f32[128,128]{1,0:T(8,128)} %convolution_bitcast_fusion.36) | copy-start | bytes 196612
  341.9 22.2 %copy-start.132 = (f32[128,128]{1,0:T(8,128)S(1)}, f32[128,128]{1,0:T(8,128)}, u32[]{:S(2)}) copy-start(f32[128,128]{1,0:T(8,128)} %convolution_bitcast_fusion.27) | copy-start | bytes 196612
  360.0 9.5 %all-to-all-start.4 = ((bf16[4,2,15360]{2,1,0:T(2,128)(2,1)}), bf16[4,2,15360]{2,1,0:T(2,128)(2,1)S(1)}, u32[]{:S(2)}, u32[]{:S(2)}) async-start(bf16[4,2,15360]{2,1,0:T(2,128)(2,1)} %reshape.1664), calls=%async_computation.4 | async-start | bytes 491520 | tf_op jit(solution)/shard_map/all_to_all | solution.py:104
  401.0 9.7 %all-to-all-start.5 = ((bf16[8,6,2560]{2,1,0:T(8,128)(2,1)}), bf16[8,6,2560]{2,1,0:T(8,128)(2,1)}, u32[]{:S(2)}, u32[]{:S(2)}) async-start(bf16[8,6,2560]{2,1,0:T(8,128)(2,1)} %reshape.1657), calls=%async_computation.5 | async-start | bytes 655360 | tf_op jit(solution)/shard_map/all_to_all | solution.py:109
  425.8 22.6 %copy-start.23 = (bf16[128,128,1,1]{1,0,2,3:T(8,128)(2,1)S(1)}, bf16[128,128,1,1]{1,0,2,3:T(8,128)(2,1)}, u32[]{:S(2)}) copy-start(bf16[128,128,1,1]{1,0,2,3:T(8,128)(2,1)} %copy-done.21) | copy-start | bytes 98308
  425.8 22.9 %copy-start.18 = (bf16[128,128,1,1]{1,0,2,3:T(8,128)(2,1)S(1)}, bf16[128,128,1,1]{1,0,2,3:T(8,128)(2,1)}, u32[]{:S(2)}) copy-start(bf16[128,128,1,1]{1,0,2,3:T(8,128)(2,1)} %copy-done.16) | copy-start | bytes 98308
  428.3 21.9 %copy-start.8 = (bf16[128,128,1,1]{1,0,2,3:T(8,128)(2,1)S(1)}, bf16[128,128,1,1]{1,0,2,3:T(8,128)(2,1)}, u32[]{:S(2)}) copy-start(bf16[128,128,1,1]{1,0,2,3:T(8,128)(2,1)} %copy-done.6) | copy-start | bytes 98308
  429.4 57.5 %all-to-all-start.12 = ((bf16[4,2,6,2560]{3,1,2,0:T(2,128)(2,1)}), bf16[4,2,6,2560]{3,1,2,0:T(2,128)(2,1)}, u32[]{:S(2)}, u32[]{:S(2)}) async-start(bf16[4,2,6,2560]{3,1,2,0:T(2,128)(2,1)} %pad_maximum_fusion.2), calls=%async_computation.12 | async-start | bytes 491520 | tf_op jit(solution)/shard_map/all_to_all | solution.py:8
  456.9 30.0 %copy-start.104 = (bf16[2,6,10240]{2,0,1:T(2,128)(2,1)}, bf16[2,6,10240]{2,0,1:T(2,128)(2,1)S(1)}, u32[]{:S(2)}) copy-start(bf16[2,6,10240]{2,0,1:T(2,128)(2,1)S(1)} %add_convert_fusion.3) | copy-start | bytes 737284
  456.9 11.7 %collective-permute-start.2 = (bf16[2,6,10240]{2,0,1:T(2,128)(2,1)S(1)}, bf16[2,6,10240]{2,0,1:T(2,128)(2,1)S(1)}, u32[]{:S(2)}, u32[]{:S(2)}) collective-permute-start(bf16[2,6,10240]{2,0,1:T(2,128)(2,1)S(1)} %add_convert_fusion.3), channel_id=1, source_target_pairs={{8,0},{16,8},{24,16},{9,1},{17,9},{25,17},{10,2},{18,10},{26,18},{... | collective-permute-start | bytes 737288 | tf_op jit(solution)/shard_map/ppermute | solution.py:21
  468.8 22.2 %copy-start.119 = (bf16[2,6,80,128]{3,2,1,0:T(8,128)(2,1)S(1)}, bf16[2,6,80,128]{3,2,1,0:T(8,128)(2,1)}, u32[]{:S(2)}) copy-start(bf16[2,6,80,128]{3,2,1,0:T(8,128)(2,1)} %copy-done.118) | copy-start | bytes 737284
  468.9 22.2 %copy-start.123 = (bf16[2,6,80,128]{3,2,0,1:T(8,128)(2,1)S(1)}, bf16[2,6,80,128]{3,2,0,1:T(8,128)(2,1)}, u32[]{:S(2)}) copy-start(bf16[2,6,80,128]{3,2,0,1:T(8,128)(2,1)} %reshape.1436) | copy-start | bytes 737284
  486.9 9.5 %all-to-all-start.6 = ((bf16[4,2,15360]{2,1,0:T(2,128)(2,1)}), bf16[4,2,15360]{2,1,0:T(2,128)(2,1)S(1)}, u32[]{:S(2)}, u32[]{:S(2)}) async-start(bf16[4,2,15360]{2,1,0:T(2,128)(2,1)} %reshape.1666), calls=%async_computation.6 | async-start | bytes 491520 | tf_op jit(solution)/shard_map/all_to_all | solution.py:104
  527.9 9.9 %all-to-all-start.7 = ((bf16[8,6,2560]{2,1,0:T(8,128)(2,1)}), bf16[8,6,2560]{2,1,0:T(8,128)(2,1)}, u32[]{:S(2)}, u32[]{:S(2)}) async-start(bf16[8,6,2560]{2,1,0:T(8,128)(2,1)} %reshape.1658), calls=%async_computation.7 | async-start | bytes 655360 | tf_op jit(solution)/shard_map/all_to_all | solution.py:109
  554.7 22.2 %copy-start.24 = (bf16[128,128,1,1]{1,0,2,3:T(8,128)(2,1)S(1)}, bf16[128,128,1,1]{1,0,2,3:T(8,128)(2,1)}, u32[]{:S(2)}) copy-start(bf16[128,128,1,1]{1,0,2,3:T(8,128)(2,1)} %copy-done.21) | copy-start | bytes 98308
  554.7 22.5 %copy-start.19 = (bf16[128,128,1,1]{1,0,2,3:T(8,128)(2,1)S(1)}, bf16[128,128,1,1]{1,0,2,3:T(8,128)(2,1)}, u32[]{:S(2)}) copy-start(bf16[128,128,1,1]{1,0,2,3:T(8,128)(2,1)} %copy-done.16) | copy-start | bytes 98308
  557.2 21.5 %copy-start.9 = (bf16[128,128,1,1]{1,0,2,3:T(8,128)(2,1)S(1)}, bf16[128,128,1,1]{1,0,2,3:T(8,128)(2,1)}, u32[]{:S(2)}) copy-start(bf16[128,128,1,1]{1,0,2,3:T(8,128)(2,1)} %copy-done.6) | copy-start | bytes 98308
  558.3 54.9 %all-to-all-start.13 = ((bf16[4,2,6,2560]{3,1,2,0:T(2,128)(2,1)}), bf16[4,2,6,2560]{3,1,2,0:T(2,128)(2,1)}, u32[]{:S(2)}, u32[]{:S(2)}) async-start(bf16[4,2,6,2560]{3,1,2,0:T(2,128)(2,1)} %pad_maximum_fusion.3), calls=%async_computation.13 | async-start | bytes 491520 | tf_op jit(solution)/shard_map/all_to_all | solution.py:8
  583.6 29.7 %copy-start.105 = (bf16[2,6,10240]{2,0,1:T(2,128)(2,1)}, bf16[2,6,10240]{2,0,1:T(2,128)(2,1)S(1)}, u32[]{:S(2)}) copy-start(bf16[2,6,10240]{2,0,1:T(2,128)(2,1)S(1)} %add_convert_fusion.2) | copy-start | bytes 737284
  583.6 11.3 %collective-permute-start.3 = (bf16[2,6,10240]{2,0,1:T(2,128)(2,1)S(1)}, bf16[2,6,10240]{2,0,1:T(2,128)(2,1)S(1)}, u32[]{:S(2)}, u32[]{:S(2)}) collective-permute-start(bf16[2,6,10240]{2,0,1:T(2,128)(2,1)S(1)} %add_convert_fusion.2), channel_id=1, source_target_pairs={{8,0},{16,8},{24,16},{9,1},{17,9},{25,17},{10,2},{18,10},{26,18},{... | collective-permute-start | bytes 737288 | tf_op jit(solution)/shard_map/ppermute | solution.py:21
  595.2 22.3 %copy-start.129 = (f32[128,128]{1,0:T(8,128)S(1)}, f32[128,128]{1,0:T(8,128)}, u32[]{:S(2)}) copy-start(f32[128,128]{1,0:T(8,128)} %convolution_bitcast_fusion.18) | copy-start | bytes 196612
  595.2 22.2 %copy-start.131 = (f32[128,128]{1,0:T(8,128)S(1)}, f32[128,128]{1,0:T(8,128)}, u32[]{:S(2)}) copy-start(f32[128,128]{1,0:T(8,128)} %convolution_bitcast_fusion.9) | copy-start | bytes 196612
  613.3 9.5 %all-to-all-start.8 = ((bf16[4,2,15360]{2,1,0:T(2,128)(2,1)}), bf16[4,2,15360]{2,1,0:T(2,128)(2,1)S(1)}, u32[]{:S(2)}, u32[]{:S(2)}) async-start(bf16[4,2,15360]{2,1,0:T(2,128)(2,1)} %reshape.1668), calls=%async_computation.8 | async-start | bytes 491520 | tf_op jit(solution)/shard_map/all_to_all | solution.py:104
  649.4 9.1 %all-to-all-start.9 = ((bf16[8,6,2560]{2,1,0:T(8,128)(2,1)}), bf16[8,6,2560]{2,1,0:T(8,128)(2,1)S(1)}, u32[]{:S(2)}, u32[]{:S(2)}) async-start(bf16[8,6,2560]{2,1,0:T(8,128)(2,1)} %reshape.1659), calls=%async_computation.9 | async-start | bytes 655360 | tf_op jit(solution)/shard_map/all_to_all | solution.py:109
  675.8 26.1 %copy-start.25 = (bf16[128,128,1,1]{1,0,2,3:T(8,128)(2,1)S(1)}, bf16[128,128,1,1]{1,0,2,3:T(8,128)(2,1)}, u32[]{:S(2)}) copy-start(bf16[128,128,1,1]{1,0,2,3:T(8,128)(2,1)} %copy-done.21) | copy-start | bytes 98308
  677.1 25.0 %copy-start.20 = (bf16[128,128,1,1]{1,0,2,3:T(8,128)(2,1)S(1)}, bf16[128,128,1,1]{1,0,2,3:T(8,128)(2,1)}, u32[]{:S(2)}) copy-start(bf16[128,128,1,1]{1,0,2,3:T(8,128)(2,1)} %copy-done.16) | copy-start | bytes 98308
  677.1 33.6 %all-to-all-start.14 = ((bf16[4,2,6,2560]{3,1,2,0:T(2,128)(2,1)}), bf16[4,2,6,2560]{3,1,2,0:T(2,128)(2,1)}, u32[]{:S(2)}, u32[]{:S(2)}) async-start(bf16[4,2,6,2560]{3,1,2,0:T(2,128)(2,1)} %pad_maximum_fusion.4), calls=%async_computation.14 | async-start | bytes 491520 | tf_op jit(solution)/shard_map/all_to_all | solution.py:8
  681.3 64.7 %all-reduce.17.cloned.1.call-start = ((), (), s32[]{:S(2)}) async-start(), calls=%async_computation.15 | async-start | bytes 589824 | tf_op jit(solution)/shard_map/psum | solution.py:143
  (109 other events, 1033.9 us)
Sparse Core Ops, SparseCore 0:
  691.5 54.4 all-reduce.16
